TPU v7x, 32 devices: a whole 2x2x4 slice. The times are simulated.
32 devices in a mesh: ctx: 4 (over z), exp: 8 (over y, x, core).
Axes of the slice: x: 2, y: 2, z: 4, core: 2. Of those that a mesh axis runs over, the one named last changes fastest.
Arguments:
- query_rows: bfloat16 [768, 1024], P('ctx', 'exp'), may hold values from -6 to 6
- key_rows: bfloat16 [768, 1024], P('ctx', 'exp'), may hold values from -6 to 6
- value_rows: bfloat16 [768, 1024], P('ctx', 'exp'), may hold values from -6 to 6
- log_decay: float32 [8, 768], P('exp', 'ctx'), may hold values from -1 to 0
- residual: bfloat16 [768, 3072], P(('ctx', 'exp')), may hold values from -20 to 20
- norm_gain: float32 [3072], replicated, may hold values from 0.1 to 1.9
- out_grad: bfloat16 [768, 3072], P(('ctx', 'exp')), may hold values from -6 to 6
- experts_of: int32 [768, 2], P(('ctx', 'exp')), may hold values from 0 to 7, all different within a row; in each aligned block of 24 rows (0 to 23, 24 to 47, ...) at most 9 rows name the same one
- route_weight: float32 [768, 2], P(('ctx', 'exp')), may hold values from 0.1 to 0.9
- output_weight: bfloat16 [1024, 3072], P('exp'), may hold values from -0.1875 to 0.1875
- expert_gate: bfloat16 [8, 3072, 4608], P('exp', None, 'ctx'), may hold values from -0.109375 to 0.109375
- expert_up: bfloat16 [8, 3072, 4608], P('exp', None, 'ctx'), may hold values from -0.109375 to 0.109375
- expert_down: bfloat16 [8, 4608, 3072], P('exp', 'ctx'), may hold values from -0.09375 to 0.09375
Outputs:
- query_grad: bfloat16 [768, 1024], P('ctx', 'exp')
- key_grad: bfloat16 [768, 1024], P('ctx', 'exp')
- value_grad: bfloat16 [768, 1024], P('ctx', 'exp')
Inputs may be any that keep to these rules, and one draw needn't show every extreme that they name: `experts_of`: in each aligned block of 24 tokens (the tokens of one device) no expert is named by more than 9 tokens, a bound that some block reaches; a token's two experts differ.
All inputs are finite; a program needn't handle non-finite values.
Results may differ from a plain program's by a relative error of at most 0.017.
Values may be sent and summed in bfloat16 or wider, within the bound.
A program may use at most 128 MiB of HBM per device.

v0:
```python
import math

import jax
import jax.numpy as jnp
from jax import lax
from jax.sharding import PartitionSpec as P


def prefix(part, axis, combine, identity, reverse):
    count = lax.axis_size(axis)
    place = lax.axis_index(axis)
    ahead = count - 1 - place if reverse else place
    gathered = jax.tree.map(lambda a: lax.all_gather(a, axis), part)
    state = jax.tree.map(lambda a, e: jnp.zeros_like(a) + jnp.asarray(e, a.dtype), part, identity)

    def one(turn, state):
        source = count - 1 - turn if reverse else turn
        return combine(
            state, jax.tree.map(lambda a: lax.dynamic_index_in_dim(a, source, 0, False), gathered)
        )

    return lax.fori_loop(0, ahead, one, state)


def normalize(residual, norm_gain):
    residual_f = residual.astype(jnp.float32)
    factor = lax.rsqrt(jnp.mean(residual_f * residual_f, axis=-1, keepdims=True) + 1e-05)
    return (residual_f, factor, (residual_f * factor * norm_gain).astype(jnp.bfloat16))


def slot_table(experts_of, count, capacity):
    flat_ids = experts_of.reshape(-1)
    matches = (flat_ids[:, None] == jnp.arange(count, dtype=jnp.int32)[None, :]).astype(jnp.int32)
    before = jnp.cumsum(matches, axis=0, dtype=jnp.int32) - matches
    target = flat_ids * capacity + jnp.sum(before * matches, axis=1, dtype=jnp.int32)
    slots = jnp.arange(count * capacity, dtype=jnp.int32)
    return (slots[:, None] == target[None, :]).astype(jnp.bfloat16)


def expert_rows(row_block, gate_mat, up_mat, down_mat):
    features = gate_mat.shape[0]
    row_input = row_block[:, :features]
    row_grad = row_block[:, features:]
    gate_pre = jnp.dot(row_input, gate_mat, preferred_element_type=jnp.float32)
    up_pre = jnp.dot(row_input, up_mat, preferred_element_type=jnp.float32)
    hidden_grad = lax.dot_general(
        row_grad, down_mat, (((1,), (1,)), ((), ())), preferred_element_type=jnp.float32
    )
    gate_sig = jax.nn.sigmoid(gate_pre)
    gate_grad = (hidden_grad * up_pre * gate_sig * (1.0 + gate_pre * (1.0 - gate_sig))).astype(
        jnp.bfloat16
    )
    up_grad = (hidden_grad * gate_pre * gate_sig).astype(jnp.bfloat16)
    first = lax.dot_general(
        gate_grad, gate_mat, (((1,), (1,)), ((), ())), preferred_element_type=jnp.float32
    )
    second = lax.dot_general(
        up_grad, up_mat, (((1,), (1,)), ((), ())), preferred_element_type=jnp.float32
    )
    return first + second


def block_terms(query_part, key_part, value_part, grad_part, log_steps, score_scale):
    levels = jnp.cumsum(log_steps)
    block_total = levels[-1]
    from_start = jnp.exp(levels)
    to_end = jnp.exp(block_total - levels)
    key_state = lax.dot_general(
        key_part.astype(jnp.float32) * to_end[:, None],
        value_part.astype(jnp.float32),
        (((0,), (0,)), ((), ())),
        precision=lax.Precision.HIGHEST,
    )
    adjoint = score_scale * lax.dot_general(
        query_part.astype(jnp.float32) * from_start[:, None],
        grad_part.astype(jnp.float32),
        (((0,), (0,)), ((), ())),
        precision=lax.Precision.HIGHEST,
    )
    return (levels, jnp.exp(block_total), key_state, adjoint)


def block_grads(
    query_part, key_part, value_part, grad_part, levels, state_in, adjoint_out, score_scale
):
    block_total = levels[-1]
    from_start = jnp.exp(levels)
    to_end = jnp.exp(block_total - levels)
    token_position = jnp.arange(levels.shape[0], dtype=jnp.int32)
    causal = token_position[:, None] >= token_position[None, :]
    fading = jnp.exp(jnp.where(causal, levels[:, None] - levels[None, :], -jnp.inf))
    scores = lax.dot_general(
        query_part, key_part, (((1,), (1,)), ((), ())), preferred_element_type=jnp.float32
    )
    attn_probs = (score_scale * scores * fading).astype(jnp.bfloat16)
    grad_scores = lax.dot_general(
        grad_part, value_part, (((1,), (1,)), ((), ())), preferred_element_type=jnp.float32
    )
    pull_weights = (score_scale * grad_scores * fading).astype(jnp.bfloat16)
    grad_f = grad_part.astype(jnp.float32)
    query_out = jnp.dot(pull_weights, key_part, preferred_element_type=jnp.float32)
    query_out = query_out + score_scale * from_start[:, None] * lax.dot_general(
        grad_f, state_in, (((1,), (1,)), ((), ())), precision=lax.Precision.HIGHEST
    )
    key_out = lax.dot_general(
        pull_weights, query_part, (((0,), (0,)), ((), ())), preferred_element_type=jnp.float32
    )
    key_out = key_out + to_end[:, None] * lax.dot_general(
        value_part.astype(jnp.float32),
        adjoint_out,
        (((1,), (1,)), ((), ())),
        precision=lax.Precision.HIGHEST,
    )
    value_out = lax.dot_general(
        attn_probs, grad_part, (((0,), (0,)), ((), ())), preferred_element_type=jnp.float32
    )
    value_out = value_out + to_end[:, None] * jnp.dot(
        key_part.astype(jnp.float32), adjoint_out, precision=lax.Precision.HIGHEST
    )
    return (
        query_out.astype(jnp.bfloat16),
        key_out.astype(jnp.bfloat16),
        value_out.astype(jnp.bfloat16),
    )


def chain_link(earlier, following):
    return (earlier[0] * following[0], following[0] * earlier[1] + following[1])


def body(
    query_rows,
    key_rows,
    value_rows,
    log_decay,
    residual,
    norm_gain,
    out_grad,
    experts_of,
    route_weight,
    output_weight,
    expert_gate,
    expert_up,
    expert_down,
):
    ctx_count = lax.axis_size("ctx")
    exp_count = lax.axis_size("exp")
    token_count = residual.shape[0]
    features = residual.shape[1]
    capacity = max(2, 3 * token_count // exp_count)
    residual_f, factor, expert_input = normalize(residual, norm_gain)
    slot_onehot = slot_table(experts_of, exp_count, capacity)
    routed = (route_weight[:, :, None] * out_grad.astype(jnp.float32)[:, None, :]).astype(
        jnp.bfloat16
    )
    inputs = jnp.broadcast_to(expert_input[:, None, :], routed.shape)
    packed = jnp.concatenate([inputs, routed], axis=-1).reshape(2 * token_count, 2 * features)
    outgoing = jnp.dot(slot_onehot, packed, preferred_element_type=jnp.float32).astype(jnp.bfloat16)
    outgoing = outgoing.reshape(exp_count, capacity, 2 * features)
    gate_mat = expert_gate[0]
    up_mat = expert_up[0]
    down_mat = expert_down[0]
    arrived = lax.all_to_all(outgoing, "exp", split_axis=0, concat_axis=0, tiled=True).reshape(
        exp_count * capacity, 2 * features
    )
    partials = expert_rows(
        lax.all_gather(arrived, "ctx", axis=0, tiled=True), gate_mat, up_mat, down_mat
    )
    partials = partials.reshape(ctx_count, exp_count, capacity, features)
    summed = lax.psum_scatter(
        partials.astype(jnp.bfloat16), "ctx", scatter_dimension=0, tiled=True
    ).astype(jnp.float32)
    returned = lax.all_to_all(
        summed[0].astype(jnp.bfloat16), "exp", split_axis=0, concat_axis=0, tiled=True
    )
    per_row = lax.dot_general(
        slot_onehot,
        returned.reshape(exp_count * capacity, features),
        (((0,), (0,)), ((), ())),
        preferred_element_type=jnp.float32,
    )
    moe_grad = jnp.sum(per_row.reshape(token_count, 2, features), axis=1)
    scaled = norm_gain * moe_grad
    unit_rows = residual_f * factor
    total_grad = out_grad.astype(jnp.float32) + factor * (
        scaled - unit_rows * jnp.mean(unit_rows * scaled, axis=-1, keepdims=True)
    )
    resid_grad = total_grad.astype(jnp.bfloat16)
    attn_grad = lax.dot_general(
        lax.all_gather(resid_grad, "exp", axis=0, tiled=True),
        output_weight,
        (((1,), (1,)), ((), ())),
        preferred_element_type=jnp.float32,
    ).astype(jnp.bfloat16)
    block_len = query_rows.shape[0]
    head_size = query_rows.shape[1]
    score_scale = 1.0 / math.sqrt(head_size * block_len * ctx_count)
    levels, block_gain, key_state, adjoint = block_terms(
        query_rows, key_rows, value_rows, attn_grad, log_decay[0], score_scale
    )
    zero_state = jnp.zeros((head_size, head_size), jnp.float32)
    identity = (jnp.ones((), jnp.float32), zero_state)
    state_pair = prefix((block_gain, key_state), "ctx", chain_link, identity, False)
    adjoint_pair = prefix((block_gain, adjoint), "ctx", chain_link, identity, True)
    state_in = state_pair[1]
    adjoint_out = adjoint_pair[1]
    return block_grads(
        query_rows, key_rows, value_rows, attn_grad, levels, state_in, adjoint_out, score_scale
    )


def solution(mesh):
    placed = (
        P("ctx", "exp"),
        P("ctx", "exp"),
        P("ctx", "exp"),
        P("exp", "ctx"),
        P(("ctx", "exp"), None),
        P(),
        P(("ctx", "exp"), None),
        P(("ctx", "exp"), None),
        P(("ctx", "exp"), None),
        P("exp", None),
        P("exp", None, "ctx"),
        P("exp", None, "ctx"),
        P("exp", "ctx", None),
    )
    return jax.shard_map(
        body,
        mesh=mesh,
        in_specs=placed,
        out_specs=(P("ctx", "exp"), P("ctx", "exp"), P("ctx", "exp")),
        check_vma=False,
    )
```

profile of v0, /device:TPU:0, one launch (start us, length us, event | category | flops | bytes accessed | tf_op | source)
XLA Modules:
  0.0 284.4 jit_solution(9164926707984191546)
XLA Ops:
  7.2 0.8 copy.18
  8.5 1.1 fusion.62
  9.6 1.0 fusion.56
  10.9 1.1 mul.198
  11.9 0.4 mul.199
  12.7 0.4 convolution_convert_fusion
  13.0 0.4 reshape.99
  13.5 26.1 %all_to_all.10 = bf16[8,9,6144]{2,1,0:T(8,128)(2,1)} all-to-all(bf16[8,9,6144]{2,1,0:T(8,128)(2,1)S(1)} %reshape.99), channel_id=1, replica_groups=mesh['ctx'=4,'exp'=8] {'exp'}, dimensions={0} | all-to-all | bytes 1769472 | tf_op jit(solution)/shard_map/all_to_all | solution.py:163
  39.5 2.7 reshape.100
  42.3 0.2 reduce-scatter.2.cloned.1.call-start
  42.5 69.3 %all-gather.5.cloned.1.call-done = bf16[288,6144]{1,0:T(8,128)(2,1)} async-done(((bf16[72,6144]{1,0:T(8,128)(2,1)}), bf16[288,6144]{1,0:T(8,128)(2,1)}) %all-gather.5.cloned.1.call-update) | async-done | bytes 3538960 | tf_op jit(solution)/shard_map/all_gather | solution.py:167
  111.8 6.1 %fusion.2 = f32[288,1152]{1,0:T(8,128)S(1)} fusion(bf16[1,3072,1152]{2,1,0:T(8,128)(2,1)} %param.27, bf16[288,6144]{1,0:T(8,128)(2,1)} %all-gather.5.cloned.1.call-done), kind=kOutput, calls=%fused_computation.4 | convolution fusion | flops 2038431744 | bytes 10174464 | tf_op jit(solution)/shard_map/dot_general | solution.py:44
  118.0 6.0 %fusion.8 = f32[288,1152]{1,0:T(8,128)S(1)} fusion(bf16[1,1152,3072]{2,1,0:T(8,128)(2,1)} %param.29, bf16[288,6144]{1,0:T(8,128)(2,1)S(1)} %copy-done.9), kind=kOutput, calls=%fused_computation.10 | convolution fusion | flops 2038431744 | bytes 10174464 | tf_op jit(solution)/shard_map/dot_general | solution.py:46
  124.0 1.1 copy-done.11
  125.1 12.7 %fusion = f32[288,3072]{1,0:T(8,128)} fusion(bf16[1,3072,1152]{2,1,0:T(8,128)(2,1)} %param.27, f32[288,1152]{1,0:T(8,128)S(1)} %fusion.8, bf16[1,3072,1152]{2,1,0:T(8,128)(2,1)} %param.28, bf16[288,6144]{1,0:T(8,128)(2,1)} %all-gather.5.cloned.1.call-done, f32[288,1152]{1,0:T(8,128)S(1)} %fusion.2), kind=kOutput, calls=%fused_computation.2 | convolution fusion | flops 4080181248 | bytes 22118400 | tf_op jit(solution)/shard_map/dot_general | solution.py:54
  137.8 7.4 %fusion.13 = bf16[288,3072]{1,0:T(8,128)(2,1)S(1)} fusion(f32[288,3072]{1,0:T(8,128)} %fusion, bf16[1,3072,1152]{2,1,0:T(8,128)(2,1)} %param.28, f32[288,1152]{1,0:T(8,128)} %copy-done.11, f32[288,1152]{1,0:T(8,128)} %copy-done.12), kind=kOutput, calls=%fused_computation.14 | convolution fusion | flops 2042191872 | bytes 15040512 | tf_op jit(solution)/shard_map/dot_general | solution.py:57
  145.1 2.4 convert_element_type.79
  147.6 59.0 %reduce-scatter.2.cloned.1.call-done = bf16[1,8,9,3072]{3,2,1,0:T(8,128)(2,1)} async-done(((bf16[4,8,9,3072]{3,2,1,0:T(8,128)(2,1)}), bf16[1,8,9,3072]{3,2,1,0:T(8,128)(2,1)}) %reduce-scatter.2.cloned.1.call-update) | async-done | bytes 442384 | tf_op jit(solution)/shard_map/reduce_scatter | solution.py:170
  206.6 3.8 %all-to-all-start.1 = ((bf16[8,9,3072]{2,1,0:T(8,128)(2,1)}), bf16[8,9,3072]{2,1,0:T(8,128)(2,1)S(1)}, u32[]{:S(2)}, u32[]{:S(2)}) async-start(bf16[8,9,3072]{2,1,0:T(8,128)(2,1)} %bitcast.86), calls=%async_computation.2 | async-start | bytes 1572864 | tf_op jit(solution)/shard_map/all_to_all | solution.py:173
  210.6 12.4 %all-to-all-done.1 = bf16[8,9,3072]{2,1,0:T(8,128)(2,1)S(1)} async-done(((bf16[8,9,3072]{2,1,0:T(8,128)(2,1)}), bf16[8,9,3072]{2,1,0:T(8,128)(2,1)S(1)}, u32[]{:S(2)}, u32[]{:S(2)}) %all-to-all-start.1) | async-done | bytes 442400 | tf_op jit(solution)/shard_map/all_to_all | solution.py:173
  223.0 0.2 reshape.111
  223.2 0.2 convolution_reduce_fusion
  223.4 0.2 fusion.57
  223.7 0.8 fusion.61
  224.5 0.3 reduce-window.9
  225.2 0.6 slice.26
  226.5 0.6 dynamic-slice
  227.0 0.8 dynamic-update-slice
  227.8 10.7 %all-reduce.1 = f32[4]{0:T(128)S(1)} all-reduce(f32[4]{0:T(128)S(1)} %dynamic-update-slice), channel_id=1, replica_groups=mesh['ctx'=4,'exp'=8] {'ctx'}, use_global_device_ids=true, to_apply=%add.1 | all-reduce | flops 4 | bytes 32
  238.5 0.7 slice_exponential_fusion
  239.1 0.4 fusion.65
  239.5 14.0 %all-gather = f32[512,128]{1,0:T(8,128)S(1)} all-gather(f32[128,128]{1,0:T(8,128)S(1)} %fusion.65), channel_id=2, replica_groups=mesh['ctx'=4,'exp'=8] {'ctx'}, dimensions={0}, use_global_device_ids=true | all-gather | bytes 327680 | tf_op jit(solution)/shard_map/all_gather | solution.py:13
  253.6 1.7 convolution_convert_fusion.1
  255.4 0.2 fusion.33
  255.6 0.4 fusion.40
  256.0 0.2 fusion.83
  256.4 0.4 convolution_multiply_fusion.5
  256.8 14.7 %all-gather.1 = f32[512,128]{1,0:T(8,128)S(1)} all-gather(f32[128,128]{1,0:T(8,128)S(1)} %convolution_multiply_fusion.5), channel_id=3, replica_groups=mesh['ctx'=4,'exp'=8] {'ctx'}, dimensions={0}, use_global_device_ids=true | all-gather | bytes 327680 | tf_op jit(solution)/shard_map/all_gather | solution.py:13
  271.5 3.8 %while.27 = (s32[]{:T(128)}, f32[128,128]{1,0:T(8,128)S(1)}, s32[]{:T(128)}, f32[4]{0:T(128)S(1)}, f32[4,128,128]{2,1,0:T(8,128)S(1)}, /*index=5*/s32[]{:T(128)}, s32[]{:T(128)}, s32[]{:T(128)}, s32[]{:T(128)}) while((s32[]{:T(128)}, f32[128,128]{1,0:T(8,128)S(1)}, s32[]{:T(128)}, f32[4]{0:T(128)S(1)}, f32[4,128,128]{2,1,0:T(8,128)S(1)}, ...), condition=%wide.region_11.12_spmd, body=%wide.region_10.11_spmd.sunk | while | flops 32774 | bytes 196767 | solution.py:22
  271.5 0.6 dynamic_slice.35
  272.1 0.7 bitcast_add_fusion.5
  272.8 0.6 dynamic_slice.35
  273.4 0.7 bitcast_add_fusion.5
  274.1 0.6 dynamic_slice.35
  274.7 0.7 bitcast_add_fusion.5
  275.3 0.8 fusion.43
  276.2 0.8 fusion.42
  277.0 0.8 fusion.41
  (55 shorter events, 1.8 us)
Async XLA Ops:
  7.2 246.4 %copy-start = (bf16[128,3072]{1,0:T(8,128)(2,1)S(1)}, bf16[128,3072]{1,0:T(8,128)(2,1)}, u32[]{:S(2)}) copy-start(bf16[128,3072]{1,0:T(8,128)(2,1)} %param.26) | copy-start | bytes 2359300
  7.2 5.2 %copy-start.8 = (f32[24,2]{0,1:T(2,128)S(1)}, f32[24,2]{0,1:T(2,128)}, u32[]{:S(2)}) copy-start(f32[24,2]{0,1:T(2,128)} %param.25) | copy-start | bytes 580
  7.2 104.6 %all-gather.5.cloned.1.call-start = ((), (), s32[]{:S(2)}) async-start(), calls=%async_computation.3 | async-start | bytes 4423680 | tf_op jit(solution)/shard_map/all_gather | solution.py:167
  42.3 164.3 %reduce-scatter.2.cloned.1.call-start = ((), (), s32[]{:S(2)}) async-start(), calls=%async_computation.4 | async-start | bytes 3932160 | tf_op jit(solution)/shard_map/reduce_scatter | solution.py:170
  111.8 6.1 %copy-start.9 = (bf16[288,6144]{1,0:T(8,128)(2,1)S(1)}, bf16[288,6144]{1,0:T(8,128)(2,1)}, u32[]{:S(2)}) copy-start(bf16[288,6144]{1,0:T(8,128)(2,1)} %all-gather.5.cloned.1.call-done) | copy-start | bytes 10616836
  117.9 6.0 %copy-start.12 = (f32[288,1152]{1,0:T(8,128)}, f32[288,1152]{1,0:T(8,128)S(1)}, u32[]{:S(2)}) copy-start(f32[288,1152]{1,0:T(8,128)S(1)} %fusion.2) | copy-start | bytes 3981316
  124.0 1.1 copy-start.11
  206.6 16.8 %copy-start.1 = (bf16[24,3072]{1,0:T(8,128)(2,1)S(1)}, bf16[24,3072]{1,0:T(8,128)(2,1)}, u32[]{:S(2)}) copy-start(bf16[24,3072]{1,0:T(8,128)(2,1)} %param.21) | copy-start | bytes 442372
  206.6 16.8 %copy-start.6 = (f32[3072]{0:T(1024)S(1)}, f32[3072]{0:T(1024)}, u32[]{:S(2)}) copy-start(f32[3072]{0:T(1024)} %param.22) | copy-start | bytes 36868
  206.6 17.1 %copy-start.2 = (bf16[24,3072]{1,0:T(8,128)(2,1)S(1)}, bf16[24,3072]{1,0:T(8,128)(2,1)}, u32[]{:S(2)}) copy-start(bf16[24,3072]{1,0:T(8,128)(2,1)} %param.23) | copy-start | bytes 442372
  206.6 16.4 %all-to-all-start.1 = ((bf16[8,9,3072]{2,1,0:T(8,128)(2,1)}), bf16[8,9,3072]{2,1,0:T(8,128)(2,1)S(1)}, u32[]{:S(2)}, u32[]{:S(2)}) async-start(bf16[8,9,3072]{2,1,0:T(8,128)(2,1)} %bitcast.86), calls=%async_computation.2 | async-start | bytes 1572864 | tf_op jit(solution)/shard_map/all_to_all | solution.py:173
  210.4 14.1 %copy-start.7 = (f32[1,192]{1,0:T(1,128)S(1)}, f32[1,192]{1,0:T(1,128)}, u32[]{:S(2)}) copy-start(f32[1,192]{1,0:T(1,128)} %param.20) | copy-start | bytes 2308
  210.4 16.1 %copy-start.10 = (u32[32]{0:T(128)S(1)}, u32[32]{0:T(128)}, u32[]{:S(2)}) copy-start(u32[32]{0:T(128)} %constant.95) | copy-start | bytes 388
  210.4 28.7 %copy-start.3 = (bf16[192,128]{1,0:T(8,128)(2,1)S(1)}, bf16[192,128]{1,0:T(8,128)(2,1)}, u32[]{:S(2)}) copy-start(bf16[192,128]{1,0:T(8,128)(2,1)} %param.18) | copy-start | bytes 147460
  210.4 28.7 %copy-start.4 = (bf16[192,128]{1,0:T(8,128)(2,1)S(1)}, bf16[192,128]{1,0:T(8,128)(2,1)}, u32[]{:S(2)}) copy-start(bf16[192,128]{1,0:T(8,128)(2,1)} %param.19) | copy-start | bytes 147460
  210.4 43.2 %all-gather.7.cloned.1.call-start = ((), (), s32[]{:S(2)}) async-start(), calls=%async_computation.5 | async-start | bytes 1327104 | tf_op jit(solution)/shard_map/all_gather | solution.py:190
  253.6 2.0 copy-start.5
Sparse Core Ops, SparseCore 0:
  42.4 69.3 all-gather.4
  147.7 58.8 reduce-scatter.1
  224.6 22.2 all-gather.6
where the time goes:
time: 285 us; the launch traced here: 284 us
  waiting for transfers between devices  141 us (49%)
  blocking collectives  65.5 us (23%)
  matrix products  38.8 us (14%)
  between operations  14.8 us (5%)
  local copies, waits for them, and re-layouts  13.7 us (5%)
  other arithmetic  6.68 us (2%)
  starting transfers between devices  4.09 us (1%)
    all_gather x1, waiting for transfers between devices, body(): lax.all_gather(arrived, 'ctx', axis=0, tiled=True)  69.3 us
    reduce_scatter x1, waiting for transfers between devices, body(): lax.psum_scatter(partials.astype(jnp.bfloat16), 'ctx', scatter_dimension=...  59 us
    all_gather x2, blocking collectives, prefix(): gathered = jax.tree.map(lambda a: lax.all_gather(a, axis), part)  28.8 us
    all_to_all x1, blocking collectives, body(): lax.all_to_all(outgoing, 'exp', split_axis=0, concat_axis=0, tiled=True)  26.1 us
    dot_general x1, matrix products, expert_rows(): lax.dot_general(gate_grad, gate_mat, (((1,), (1,)), ((), ())), preferred_...  12.7 us
    all_to_all x1, waiting for transfers between devices, body(): lax.all_to_all(summed[0].astype(jnp.bfloat16), 'exp', split_axis=0, conca...  12.4 us
    unnamed x1, blocking collectives  10.7 us
    dot_general x1, matrix products, expert_rows(): lax.dot_general(up_grad, up_mat, (((1,), (1,)), ((), ())), preferred_elem...  7.37 us
  transfers between devices with their start and end apart: 4, of which 3 were waited for; matrix products, arithmetic and copies ran while one was open for 1% of the time, Pallas kernels for 0%

commit v1 on v0

v1 whole, which is shorter than its diff:
```python
import functools
import math

import jax
import jax.numpy as jnp
from jax import lax
from jax.experimental import pallas as pl
from jax.experimental.pallas import tpu as pltpu
from jax.sharding import PartitionSpec as P

MESH = pl.DeviceIdType.MESH


def exchange_kernel(axis, n, kinds, *refs):
    k = len(kinds)
    ins, outs = refs[:k], refs[k : 2 * k]
    local_sem, send_sem, recv_sem = refs[2 * k :]
    me = lax.axis_index(axis)
    barrier = pltpu.get_barrier_semaphore()
    for s in range(1, n):
        pl.semaphore_signal(
            barrier, inc=1, device_id={axis: lax.rem(me + s, n)}, device_id_type=MESH
        )
    pl.semaphore_wait(barrier, n - 1)

    def source(i, place):
        return ins[i] if kinds[i] == "gather" else ins[i].at[place]

    def remote(i, s, place):
        peer = lax.rem(me + s, n)
        return pltpu.make_async_remote_copy(
            src_ref=source(i, peer),
            dst_ref=outs[i].at[place],
            send_sem=send_sem.at[i, s - 1],
            recv_sem=recv_sem.at[i, s - 1],
            device_id={axis: peer},
            device_id_type=MESH,
        )

    sent = [remote(i, s, me) for i in range(k) for s in range(1, n)]
    for copy in sent:
        copy.start()
    own = [
        pltpu.make_async_copy(source(i, me), outs[i].at[me], local_sem.at[i]) for i in range(k)
    ]
    for copy in own:
        copy.start()
    for copy in own:
        copy.wait()
    for i in range(k):
        for s in range(1, n):
            remote(i, s, lax.rem(me - s + n, n)).wait_recv()
    for copy in sent:
        copy.wait_send()


def exchange(axis, collective_id, arrays, kinds):
    n = lax.axis_size(axis)
    k = len(arrays)
    shapes = [
        jax.ShapeDtypeStruct((n,) + a.shape if kind == "gather" else a.shape, a.dtype)
        for a, kind in zip(arrays, kinds)
    ]
    return pl.pallas_call(
        functools.partial(exchange_kernel, axis, n, kinds),
        out_shape=shapes,
        in_specs=[pl.BlockSpec(memory_space=pl.ANY)] * k,
        out_specs=[pl.BlockSpec(memory_space=pl.ANY)] * k,
        scratch_shapes=[
            pltpu.SemaphoreType.DMA((k,)),
            pltpu.SemaphoreType.DMA((k, n - 1)),
            pltpu.SemaphoreType.DMA((k, n - 1)),
        ],
        compiler_params=pltpu.CompilerParams(collective_id=collective_id, has_side_effects=True),
    )(*arrays)


def dot_bt(a, b):
    return lax.dot_general(a, b, (((1,), (1,)), ((), ())), preferred_element_type=jnp.float32)


def expert_kernel(x_ref, g_ref, gate_ref, up_ref, down_ref, out_ref, acc_ref):
    step = pl.program_id(0)
    gate_mat = gate_ref[0]
    up_mat = up_ref[0]
    gate_pre = jnp.dot(x_ref[...], gate_mat, preferred_element_type=jnp.float32)
    up_pre = jnp.dot(x_ref[...], up_mat, preferred_element_type=jnp.float32)
    hidden_grad = dot_bt(g_ref[...], down_ref[0])
    gate_sig = 1.0 / (1.0 + jnp.exp(-gate_pre))
    gate_grad = (hidden_grad * up_pre * gate_sig * (1.0 + gate_pre * (1.0 - gate_sig))).astype(
        jnp.bfloat16
    )
    up_grad = (hidden_grad * gate_pre * gate_sig).astype(jnp.bfloat16)
    term = dot_bt(gate_grad, gate_mat) + dot_bt(up_grad, up_mat)

    @pl.when(step == 0)
    def _():
        acc_ref[...] = term

    @pl.when(step > 0)
    def _():
        acc_ref[...] += term

    @pl.when(step == pl.num_programs(0) - 1)
    def _():
        count, _, half = out_ref.shape
        rows = acc_ref.shape[0] // count
        for d in range(count):
            part = acc_ref[d * rows : (d + 1) * rows, :]
            out_ref[d] = jnp.concatenate([part[:, :half], part[:, half:]], axis=0).astype(
                jnp.bfloat16
            )


def expert_rows(x, g, gate, up, down, count):
    rows, features = x.shape
    hidden = gate.shape[2]
    tile = next((t for t in (384, 256, 128) if hidden % t == 0), hidden)
    half = features // 2
    return pl.pallas_call(
        expert_kernel,
        grid=(hidden // tile,),
        out_shape=jax.ShapeDtypeStruct((count, 2 * (rows // count), half), jnp.bfloat16),
        in_specs=[
            pl.BlockSpec((rows, features), lambda f: (0, 0)),
            pl.BlockSpec((rows, features), lambda f: (0, 0)),
            pl.BlockSpec((1, features, tile), lambda f: (0, 0, f)),
            pl.BlockSpec((1, features, tile), lambda f: (0, 0, f)),
            pl.BlockSpec((1, tile, features), lambda f: (0, f, 0)),
        ],
        out_specs=pl.BlockSpec((count, 2 * (rows // count), half), lambda f: (0, 0, 0)),
        scratch_shapes=[pltpu.VMEM((rows, features), jnp.float32)],
        compiler_params=pltpu.CompilerParams(vmem_limit_bytes=60 * 2**20),
    )(x, g, gate, up, down)


def normalize(residual, norm_gain):
    residual_f = residual.astype(jnp.float32)
    factor = lax.rsqrt(jnp.mean(residual_f * residual_f, axis=-1, keepdims=True) + 1e-05)
    return (residual_f, factor, (residual_f * factor * norm_gain).astype(jnp.bfloat16))


def block_terms(key_part, value_part, log_steps):
    place = jnp.arange(log_steps.shape[0], dtype=jnp.int32)
    levels = jnp.sum(
        jnp.where(place[:, None] >= place[None, :], log_steps[None, :], 0.0), axis=1
    )
    block_total = levels[-1]
    to_end = jnp.exp(block_total - levels)
    key_state = lax.dot_general(
        key_part.astype(jnp.float32) * to_end[:, None],
        value_part.astype(jnp.float32),
        (((0,), (0,)), ((), ())),
        precision=lax.Precision.HIGHEST,
    )
    return (levels, block_total, key_state)


def block_grads(
    query_part, key_part, value_part, grad_part, levels, state_in, adjoint_out, score_scale
):
    block_total = levels[-1]
    from_start = jnp.exp(levels)
    to_end = jnp.exp(block_total - levels)
    token_position = jnp.arange(levels.shape[0], dtype=jnp.int32)
    causal = token_position[:, None] >= token_position[None, :]
    fading = jnp.exp(jnp.where(causal, levels[:, None] - levels[None, :], -jnp.inf))
    scores = lax.dot_general(
        query_part, key_part, (((1,), (1,)), ((), ())), preferred_element_type=jnp.float32
    )
    attn_probs = (score_scale * scores * fading).astype(jnp.bfloat16)
    grad_scores = lax.dot_general(
        grad_part, value_part, (((1,), (1,)), ((), ())), preferred_element_type=jnp.float32
    )
    pull_weights = (score_scale * grad_scores * fading).astype(jnp.bfloat16)
    grad_f = grad_part.astype(jnp.float32)
    query_out = jnp.dot(pull_weights, key_part, preferred_element_type=jnp.float32)
    query_out = query_out + score_scale * from_start[:, None] * lax.dot_general(
        grad_f, state_in, (((1,), (1,)), ((), ())), precision=lax.Precision.HIGHEST
    )
    key_out = lax.dot_general(
        pull_weights, query_part, (((0,), (0,)), ((), ())), preferred_element_type=jnp.float32
    )
    key_out = key_out + to_end[:, None] * lax.dot_general(
        value_part.astype(jnp.float32),
        adjoint_out,
        (((1,), (1,)), ((), ())),
        precision=lax.Precision.HIGHEST,
    )
    value_out = lax.dot_general(
        attn_probs, grad_part, (((0,), (0,)), ((), ())), preferred_element_type=jnp.float32
    )
    value_out = value_out + to_end[:, None] * jnp.dot(
        key_part.astype(jnp.float32), adjoint_out, precision=lax.Precision.HIGHEST
    )
    return (
        query_out.astype(jnp.bfloat16),
        key_out.astype(jnp.bfloat16),
        value_out.astype(jnp.bfloat16),
    )


def body(
    query_rows,
    key_rows,
    value_rows,
    log_decay,
    residual,
    norm_gain,
    out_grad,
    experts_of,
    route_weight,
    output_weight,
    expert_gate,
    expert_up,
    expert_down,
):
    ctx_count = lax.axis_size("ctx")
    exp_count = lax.axis_size("exp")
    ctx_place = lax.axis_index("ctx")
    token_count = residual.shape[0]
    features = residual.shape[1]
    half = features // 2
    capacity = max(2, 3 * token_count // exp_count)
    depth = -(-ctx_count * capacity // 8) * 8
    slots = exp_count * depth
    all_tokens = ctx_count * token_count

    residual_f, factor, expert_input = normalize(residual, norm_gain)
    levels, block_total, key_state = block_terms(key_rows, value_rows, log_decay[0])
    meta = jnp.concatenate(
        [
            experts_of.T.astype(jnp.float32),
            route_weight.T,
            jnp.broadcast_to(block_total, (1, token_count)),
        ],
        axis=0,
    )
    meta = jnp.pad(meta, ((0, 3), (0, 128 - token_count)))
    tokens, metas, key_states = exchange(
        "ctx",
        0,
        [jnp.concatenate([expert_input, out_grad], axis=0), meta, key_state],
        ("gather", "gather", "gather"),
    )

    choice = metas[:, 0:2, :token_count].astype(jnp.int32)
    choice_by_token = jnp.transpose(choice, (0, 2, 1)).reshape(-1)
    weights = jnp.transpose(metas[:, 2:4, :token_count], (0, 2, 1)).reshape(-1)
    order = jnp.arange(2 * all_tokens, dtype=jnp.int32)
    ahead = (choice_by_token[:, None] == choice_by_token[None, :]) & (
        order[:, None] > order[None, :]
    )
    target = choice_by_token * depth + jnp.sum(ahead, axis=1, dtype=jnp.int32)
    slot_ids = jnp.arange(slots, dtype=jnp.int32)
    hits = (slot_ids[:, None] == target[None, :]).astype(jnp.float32)
    slot_weight = jnp.sum(hits * weights[None, :], axis=1)
    pick = jnp.sum(hits.reshape(exp_count, depth, ctx_count, token_count, 2), axis=-1)
    none = jnp.zeros_like(pick)
    pick_both = jnp.concatenate(
        [
            jnp.concatenate([pick, none], axis=3),
            jnp.concatenate([none, pick], axis=3),
        ],
        axis=1,
    ).reshape(2 * slots, 2 * all_tokens)
    row_scale = jnp.concatenate(
        [jnp.ones((exp_count, depth), jnp.float32), slot_weight.reshape(exp_count, depth)], axis=1
    )
    outgoing = jnp.dot(
        pick_both.astype(jnp.bfloat16),
        tokens.reshape(2 * all_tokens, features),
        preferred_element_type=jnp.float32,
    )
    outgoing = (outgoing * row_scale.reshape(-1, 1)).astype(jnp.bfloat16)
    [arrived] = exchange(
        "exp", 1, [outgoing.reshape(exp_count, 2 * depth, features)], ("swap",)
    )
    partials = expert_rows(
        arrived[:, :depth].reshape(slots, features),
        arrived[:, depth:].reshape(slots, features),
        expert_gate,
        expert_up,
        expert_down,
        exp_count,
    )
    [returned] = exchange("exp", 2, [partials], ("swap",))

    back = jnp.transpose(pick, (2, 3, 0, 1))[:, None, :, :, None, :]
    halves = jnp.eye(2, dtype=jnp.float32)[None, :, None, None, :, None]
    merge = (back * halves).reshape(2 * all_tokens, 2 * slots).astype(jnp.bfloat16)
    sums = jnp.dot(
        merge, returned.reshape(2 * slots, half), preferred_element_type=jnp.float32
    ).astype(jnp.bfloat16)
    [groups] = exchange(
        "ctx", 3, [sums.reshape(ctx_count, 2 * token_count, half)], ("swap",)
    )

    def split(a):
        return jnp.stack([a[:, :half], a[:, half:]], axis=0)

    moe_grad = jnp.sum(groups.astype(jnp.float32), axis=0).reshape(2, token_count, half)
    scaled = norm_gain.reshape(2, 1, half) * moe_grad
    unit_rows = split(residual_f * factor)
    mean = jnp.sum(unit_rows * scaled, axis=(0, 2), keepdims=True) * (1.0 / features)
    total_grad = split(out_grad.astype(jnp.float32)) + factor[None] * (scaled - unit_rows * mean)
    resid_grad = total_grad.astype(jnp.bfloat16).reshape(2 * token_count, half)
    [resid_all] = exchange("exp", 4, [resid_grad], ("gather",))
    resid_all = resid_all.reshape(exp_count, 2, token_count, half)
    block_len = query_rows.shape[0]
    head_size = query_rows.shape[1]
    attn_grad = (
        dot_bt(resid_all[:, 0].reshape(block_len, half), output_weight[:, :half])
        + dot_bt(resid_all[:, 1].reshape(block_len, half), output_weight[:, half:])
    ).astype(jnp.bfloat16)
    score_scale = 1.0 / math.sqrt(head_size * block_len * ctx_count)
    adjoint = score_scale * lax.dot_general(
        query_rows.astype(jnp.float32) * jnp.exp(levels)[:, None],
        attn_grad.astype(jnp.float32),
        (((0,), (0,)), ((), ())),
        precision=lax.Precision.HIGHEST,
    )
    [adjoints] = exchange("ctx", 5, [adjoint], ("gather",))

    totals = metas[:, 4, 0]
    place = jnp.arange(ctx_count, dtype=jnp.int32)
    between = (place[None, :] > jnp.minimum(place, ctx_place)[:, None]) & (
        place[None, :] < jnp.maximum(place, ctx_place)[:, None]
    )
    decay = jnp.exp(jnp.sum(jnp.where(between, totals[None, :], 0.0), axis=1))
    before = jnp.where(place < ctx_place, decay, 0.0)
    after = jnp.where(place > ctx_place, decay, 0.0)
    state_in = jnp.sum(before[:, None, None] * key_states, axis=0)
    adjoint_out = jnp.sum(after[:, None, None] * adjoints, axis=0)
    return block_grads(
        query_rows, key_rows, value_rows, attn_grad, levels, state_in, adjoint_out, score_scale
    )


def solution(mesh):
    placed = (
        P("ctx", "exp"),
        P("ctx", "exp"),
        P("ctx", "exp"),
        P("exp", "ctx"),
        P(("ctx", "exp"), None),
        P(),
        P(("ctx", "exp"), None),
        P(("ctx", "exp"), None),
        P(("ctx", "exp"), None),
        P("exp", None),
        P("exp", None, "ctx"),
        P("exp", None, "ctx"),
        P("exp", "ctx", None),
    )
    return jax.shard_map(
        body,
        mesh=mesh,
        in_specs=placed,
        out_specs=(P("ctx", "exp"), P("ctx", "exp"), P("ctx", "exp")),
        check_vma=False,
    )
```

time: 285 us -> 211 us (0.74)
  Pallas kernels: 0 us -> 172 us
  waiting for transfers between devices: 141 us -> 0 us
  blocking collectives: 65.5 us -> 0 us
  matrix products: 38.8 us -> 13 us
  between operations: 14.8 us -> 0.98 us
  other arithmetic: 6.68 us -> 12.9 us
  starting transfers between devices: 4.09 us -> 0 us
    pallas_call x0 -> x7, Pallas kernels: none -> 172 us  [the longest x6 148 us: exchange(): pl.pallas_call(functools.partial(exchange_kernel, axis, n, kinds), out_sh...]
    all_gather x2 -> x0, waiting for transfers between devices: 69.3 us -> none  [the longest x1 69.3 us: body(): lax.all_gather(arrived, 'ctx', axis=0, tiled=True)]
    reduce_scatter x1 -> x0, waiting for transfers between devices: 59 us -> none  [body(): lax.psum_scatter(partials.astype(jnp.bfloat16), 'ctx', scatter_dimension=...]
    all_gather x2 -> x0, blocking collectives: 28.8 us -> none  [prefix(): gathered = jax.tree.map(lambda a: lax.all_gather(a, axis), part)]
    dot_general x8 -> x5, matrix products: 34.9 us -> 7.76 us  [the longest x1 3.14 us: body(): jnp.dot(pick_both.astype(jnp.bfloat16), tokens.reshape(2 * all_tokens, fe...]
    all_to_all x1 -> x0, blocking collectives: 26.1 us -> none  [body(): lax.all_to_all(outgoing, 'exp', split_axis=0, concat_axis=0, tiled=True)]
    all_to_all x1 -> x0, waiting for transfers between devices: 12.4 us -> none  [body(): lax.all_to_all(summed[0].astype(jnp.bfloat16), 'exp', split_axis=0, conca...]
    unnamed x1 -> x0, blocking collectives: 10.7 us -> none
  transfers between devices with their start and end apart: 4 -> 0, of which waited for: 3 -> 0; matrix products, arithmetic and copies ran while one was open for 1% -> 0% of each run, Pallas kernels for 0% -> 0%
where the time goes in v1:
time: 211 us; the launch traced here: 210 us
  Pallas kernels  172 us (82%)
  matrix products  13 us (6%)
  other arithmetic  12.9 us (6%)
  local copies, waits for them, and re-layouts  11.3 us (5%)
    pallas_call x6, Pallas kernels, exchange(): pl.pallas_call(functools.partial(exchange_kernel, axis, n, kinds), out_sh...  148 us
    pallas_call x1, Pallas kernels, expert_rows(): pl.pallas_call(expert_kernel, grid=(hidden // tile,), out_shape=jax.Shape...  23.4 us
    slice x1, local copies, waits for them, and re-layouts, body(): arrived[:, depth:].reshape(slots, features)  4.36 us

profile of v1, /device:TPU:0, one launch (start us, length us, event | category | flops | bytes accessed | tf_op | source)
XLA Modules:
  0.0 210.1 jit_solution(7347887643329655379)
XLA Ops:
  0.7 1.0 fusion.20
  1.7 1.0 multiply_convert_fusion.2
  2.8 1.6 pad_maximum_fusion.1.refs_0_
  4.4 0.7 convert_bitcast_fusion.1
  5.1 0.8 select_reduce_fusion.1
  5.9 0.6 slice.45
  6.5 0.7 pad.16.clone
  7.2 0.7 maximum_maximum_fusion
  7.9 0.6 pad.9.refs_1_
  8.5 0.7 fusion.42
  9.2 1.8 fusion.32.refs_2_
  11.0 36.4 %shard_map.148 = (bf16[4,48,3072]{2,1,0:T(8,128)(2,1)}, f32[4,8,128]{2,1,0:T(8,128)}, f32[4,128,128]{2,1,0:T(8,128)}) custom-call(bf16[48,3072]{1,0:T(8,128)(2,1)} %pad_maximum_fusion.1.refs_0_, f32[8,128]{1,0:T(8,128)} %pad.9.refs_1_, f32[128,128]{1,0:T(8,128)} %fusion.32.refs_2_), custom_call_target="tpu_custom_call" | custom-call | tf_op jit(solution)/shard_map/pallas_call | solution.py:64
  47.4 0.8 slice_bitcast_fusion.4
  48.5 0.2 convert_reduce_fusion.2
  48.9 0.7 multiply_add_fusion
  49.7 0.2 convert_reduce_fusion.1
  49.8 0.2 copy.24
  50.1 0.6 multiply_convert_fusion.1
  50.7 0.9 convert_element_type.109
  51.5 0.2 fusion.16
  51.7 0.3 copy.25
  52.0 0.3 convert_element_type.110
  52.9 3.1 %multiply_convert_fusion = bf16[640,3072]{1,0:T(8,128)(2,1)} fusion(bf16[640,192]{0,1:T(8,128)(2,1)S(1)} %convert_element_type.110, bf16[192,3072]{1,0:T(8,128)(2,1)S(1)} %bitcast.97, f32[640]{0:T(1024)S(1)} %mul.251), kind=kOutput, calls=%fused_computation | convolution fusion | flops 758906880 | bytes 5360128 | tf_op jit(solution)/shard_map/dot_general | solution.py:270
  56.0 45.6 %shard_map.149 = bf16[8,80,3072]{2,1,0:T(8,128)(2,1)} custom-call(bf16[8,80,3072]{2,1,0:T(8,128)(2,1)} %bitcast.89), custom_call_target="tpu_custom_call" | custom-call | tf_op jit(solution)/shard_map/pallas_call | solution.py:64
  101.6 4.4 %fusion.40 = (bf16[8,40,3072]{2,1,0:T(8,128)(2,1)}, bf16[8,40,3072]{2,1,0:T(8,128)(2,1)}) fusion(bf16[8,80,3072]{2,1,0:T(8,128)(2,1)} %shard_map.149), kind=kLoop, calls=%fused_computation.96 | loop fusion | bytes 7864320 | tf_op jit(solution)/shard_map/slice | solution.py:281
  106.0 23.4 %shard_map.150.refs_0_ = bf16[8,80,1536]{2,1,0:T(8,128)(2,1)} custom-call(bf16[320,3072]{1,0:T(8,128)(2,1)} %bitcast.87, bf16[320,3072]{1,0:T(8,128)(2,1)} %bitcast.86, bf16[1,3072,1152]{2,1,0:T(8,128)(2,1)} %gate_ref.1, bf16[1,3072,1152]{2,1,0:T(8,128)(2,1)} %up_ref.1, bf16[1,1152,3072]{2,1,0:T(8,128)(2,1)} %down_ref.1), custom_call_target="tpu_custom_call" | custom-call | tf_op jit(solution)/shard_map/pallas_call | solution.py:120
  129.4 24.9 %shard_map.151 = bf16[8,80,1536]{2,1,0:T(8,128)(2,1)} custom-call(bf16[8,80,1536]{2,1,0:T(8,128)(2,1)} %shard_map.150.refs_0_), custom_call_target="tpu_custom_call" | custom-call | tf_op jit(solution)/shard_map/pallas_call | solution.py:64
  154.3 3.0 %convolution_convert_fusion = bf16[192,1536]{1,0:T(8,128)(2,1)} fusion(bf16[192,640]{1,0:T(8,128)(2,1)S(1)} %convert_element_type.109, bf16[640,1536]{1,0:T(8,128)(2,1)} %bitcast.85), kind=kOutput, calls=%fused_computation.1 | convolution fusion | flops 377782272 | bytes 2801664 | tf_op jit(solution)/shard_map/dot_general | solution.py:292
  157.3 15.6 %shard_map.152 = bf16[4,48,1536]{2,1,0:T(8,128)(2,1)} custom-call(bf16[4,48,1536]{2,1,0:T(8,128)(2,1)} %bitcast.94), custom_call_target="tpu_custom_call" | custom-call | tf_op jit(solution)/shard_map/pallas_call | solution.py:64
  172.9 1.2 convert_reduce_fusion
  174.2 0.2 multiply_reduce_fusion
  174.6 0.8 fusion.24.refs_0_
  175.4 14.3 %shard_map.153 = bf16[8,48,1536]{2,1,0:T(8,128)(2,1)} custom-call(bf16[48,1536]{1,0:T(8,128)(2,1)} %fusion.24.refs_0_), custom_call_target="tpu_custom_call" | custom-call | tf_op jit(solution)/shard_map/pallas_call | solution.py:64
  189.7 1.3 fusion.41
  191.1 0.3 fusion.18
  191.4 0.3 fusion.10
  191.7 0.2 fusion.2
  191.9 0.1 fusion.43
  192.1 0.8 slice_reduce_fusion
  192.9 0.2 select_reduce_fusion.2
  193.2 0.8 fusion.11
  194.1 0.2 fusion.44
  194.3 1.0 convolution_multiply_fusion.5.refs_0_
  195.3 11.7 %shard_map.154 = f32[4,128,128]{2,1,0:T(8,128)} custom-call(f32[128,128]{1,0:T(8,128)} %convolution_multiply_fusion.5.refs_0_), custom_call_target="tpu_custom_call" | custom-call | tf_op jit(solution)/shard_map/pallas_call | solution.py:64
  207.0 1.0 multiply_reduce_fusion.1
  208.0 0.8 fusion.12
  208.8 0.4 fusion.9
  209.3 0.8 fusion.13
  (43 shorter events, 1.5 us)
Async XLA Ops:
  0.6 8.6 %copy-start = (bf16[192,128]{1,0:T(8,128)(2,1)S(1)}, bf16[192,128]{1,0:T(8,128)(2,1)}, u32[]{:S(2)}) copy-start(bf16[192,128]{1,0:T(8,128)(2,1)} %param.15) | copy-start | bytes 147460
  50.6 2.2 %copy-start.7 = (bf16[4,48,3072]{2,1,0:T(8,128)(2,1)S(1)}, bf16[4,48,3072]{2,1,0:T(8,128)(2,1)}, u32[]{:S(2)}) copy-start(bf16[4,48,3072]{2,1,0:T(8,128)(2,1)} %get-tuple-element.7) | copy-start | bytes 3538948
  154.3 19.8 %copy-start.6 = (f32[3072]{0:T(1024)S(1)}, f32[3072]{0:T(1024)}, u32[]{:S(2)}) copy-start(f32[3072]{0:T(1024)} %param.18) | copy-start | bytes 36868
  157.3 16.8 %copy-start.2 = (bf16[24,3072]{1,0:T(8,128)(2,1)S(1)}, bf16[24,3072]{1,0:T(8,128)(2,1)}, u32[]{:S(2)}) copy-start(bf16[24,3072]{1,0:T(8,128)(2,1)} %param.19) | copy-start | bytes 442372
  175.4 15.7 %copy-start.1 = (bf16[128,3072]{1,0:T(8,128)(2,1)S(1)}, bf16[128,3072]{1,0:T(8,128)(2,1)}, u32[]{:S(2)}) copy-start(bf16[128,3072]{1,0:T(8,128)(2,1)} %param.22) | copy-start | bytes 2359300
  189.7 2.2 %copy-start.3 = (bf16[192,128]{1,0:T(8,128)(2,1)S(1)}, bf16[192,128]{1,0:T(8,128)(2,1)}, u32[]{:S(2)}) copy-start(bf16[192,128]{1,0:T(8,128)(2,1)} %param.14) | copy-start | bytes 147460
  191.0 2.1 copy-start.4
  191.1 3.0 %copy-start.5 = (bf16[192,128]{1,0:T(8,128)(2,1)S(1)}, bf16[192,128]{1,0:T(8,128)(2,1)}, u32[]{:S(2)}) copy-start(bf16[192,128]{1,0:T(8,128)(2,1)} %param.13) | copy-start | bytes 147460

commit v2 on v1

--- a/solution.py
+++ b/solution.py
@@ -75,12 +75,129 @@
     )(*arrays)
 
 
+def relay_kernel(axes, counts, kind, width, src, mat, scale, out, got, made, *sems):
+    local_sem, first_send, first_recv, second_send, second_recv, own_sem = sems
+    chunks = src.shape[-1] // width
+    me = [lax.axis_index(axis) for axis in axes]
+    barrier = pltpu.get_barrier_semaphore()
+    for axis, place, n in zip(axes, me, counts):
+        for s in range(1, n):
+            pl.semaphore_signal(
+                barrier, inc=1, device_id={axis: lax.rem(place + s, n)}, device_id_type=MESH
+            )
+    pl.semaphore_wait(barrier, counts[0] + counts[1] - 2)
+
+    def columns(c):
+        return pl.ds(c * width, width)
+
+    def part(c, place):
+        return src.at[:, columns(c)] if kind == "gather" else src.at[place, :, columns(c)]
+
+    def first(c, s, place):
+        peer = lax.rem(me[0] + s, counts[0])
+        return pltpu.make_async_remote_copy(
+            src_ref=part(c, peer),
+            dst_ref=got.at[place, :, columns(c)],
+            send_sem=first_send.at[c, s - 1],
+            recv_sem=first_recv.at[c, s - 1],
+            device_id={axes[0]: peer},
+            device_id_type=MESH,
+        )
+
+    def second(c, s, place):
+        peer = lax.rem(me[1] + s, counts[1])
+        return pltpu.make_async_remote_copy(
+            src_ref=made.at[peer, :, columns(c)],
+            dst_ref=out.at[place, :, columns(c)],
+            send_sem=second_send.at[c, s - 1],
+            recv_sem=second_recv.at[c, s - 1],
+            device_id={axes[1]: peer},
+            device_id_type=MESH,
+        )
+
+    sent = []
+    kept = []
+    for c in range(chunks):
+        for s in range(1, counts[0]):
+            copy = first(c, s, me[0])
+            copy.start()
+            sent.append(copy)
+        copy = pltpu.make_async_copy(
+            part(c, me[0]), got.at[me[0], :, columns(c)], local_sem.at[c]
+        )
+        copy.start()
+        kept.append(copy)
+    for c in range(chunks):
+        kept[c].wait()
+        for s in range(1, counts[0]):
+            first(c, s, lax.rem(me[0] - s + counts[0], counts[0])).wait_recv()
+        rows = got[:, :, columns(c)].reshape(-1, width)
+        term = jnp.dot(mat[...], rows, preferred_element_type=jnp.float32)
+        term = (term * scale[...]).astype(jnp.bfloat16)
+        made[:, :, columns(c)] = term.reshape(made.shape[0], made.shape[1], width)
+        for s in range(1, counts[1]):
+            copy = second(c, s, me[1])
+            copy.start()
+            sent.append(copy)
+        copy = pltpu.make_async_copy(
+            made.at[me[1], :, columns(c)], out.at[me[1], :, columns(c)], own_sem.at[c]
+        )
+        copy.start()
+        kept.append(copy)
+    for c in range(chunks):
+        kept[chunks + c].wait()
+        for s in range(1, counts[1]):
+            second(c, s, lax.rem(me[1] - s + counts[1], counts[1])).wait_recv()
+    for copy in sent:
+        copy.wait_send()
+
+
+def relay(axes, collective_id, kind, width, src, mat, scale):
+    counts = [lax.axis_size(axis) for axis in axes]
+    rows, total = src.shape[-2:]
+    out_shape = (counts[1], mat.shape[0] // counts[1], total)
+    chunks = total // width
+    vmem = pl.BlockSpec(memory_space=pltpu.VMEM)
+    return pl.pallas_call(
+        functools.partial(relay_kernel, axes, counts, kind, width),
+        out_shape=jax.ShapeDtypeStruct(out_shape, jnp.bfloat16),
+        in_specs=[pl.BlockSpec(memory_space=pl.ANY), vmem, vmem],
+        out_specs=pl.BlockSpec(memory_space=pl.ANY),
+        scratch_shapes=[
+            pltpu.VMEM((counts[0], rows, total), jnp.bfloat16),
+            pltpu.VMEM(out_shape, jnp.bfloat16),
+            pltpu.SemaphoreType.DMA((chunks,)),
+            pltpu.SemaphoreType.DMA((chunks, counts[0] - 1)),
+            pltpu.SemaphoreType.DMA((chunks, counts[0] - 1)),
+            pltpu.SemaphoreType.DMA((chunks, counts[1] - 1)),
+            pltpu.SemaphoreType.DMA((chunks, counts[1] - 1)),
+            pltpu.SemaphoreType.DMA((chunks,)),
+        ],
+        compiler_params=pltpu.CompilerParams(
+            collective_id=collective_id, has_side_effects=True, vmem_limit_bytes=40 * 2**20
+        ),
+    )(src, mat, scale)
+
+
 def dot_bt(a, b):
     return lax.dot_general(a, b, (((1,), (1,)), ((), ())), preferred_element_type=jnp.float32)
 
 
-def expert_kernel(x_ref, g_ref, gate_ref, up_ref, down_ref, out_ref, acc_ref):
+def expert_kernel(rows_ref, gate_ref, up_ref, down_ref, out_ref, x_ref, g_ref, acc_ref):
     step = pl.program_id(0)
+
+    @pl.when(step == 0)
+    def _():
+        pair = rows_ref.shape[1]
+        depth = pair // 2
+        for p in range(rows_ref.shape[0] // 2):
+            one = rows_ref[2 * p].astype(jnp.float32)
+            two = rows_ref[2 * p + 1].astype(jnp.float32)
+            for ref, cut in ((x_ref, slice(0, depth)), (g_ref, slice(depth, pair))):
+                ref[p * pair : (p + 1) * pair, :] = jnp.concatenate(
+                    [one[cut], two[cut]], axis=0
+                ).astype(jnp.bfloat16)
+
     gate_mat = gate_ref[0]
     up_mat = up_ref[0]
     gate_pre = jnp.dot(x_ref[...], gate_mat, preferred_element_type=jnp.float32)
@@ -112,26 +229,30 @@
             )
 
 
-def expert_rows(x, g, gate, up, down, count):
-    rows, features = x.shape
+def expert_rows(arrived, gate, up, down):
+    count, depth, features = arrived.shape
+    rows = count * depth // 2
     hidden = gate.shape[2]
     tile = next((t for t in (384, 256, 128) if hidden % t == 0), hidden)
-    half = features // 2
+    out_shape = (count, depth, features // 2)
     return pl.pallas_call(
         expert_kernel,
         grid=(hidden // tile,),
-        out_shape=jax.ShapeDtypeStruct((count, 2 * (rows // count), half), jnp.bfloat16),
+        out_shape=jax.ShapeDtypeStruct(out_shape, jnp.bfloat16),
         in_specs=[
-            pl.BlockSpec((rows, features), lambda f: (0, 0)),
-            pl.BlockSpec((rows, features), lambda f: (0, 0)),
+            pl.BlockSpec(arrived.shape, lambda f: (0, 0, 0)),
             pl.BlockSpec((1, features, tile), lambda f: (0, 0, f)),
             pl.BlockSpec((1, features, tile), lambda f: (0, 0, f)),
             pl.BlockSpec((1, tile, features), lambda f: (0, f, 0)),
         ],
-        out_specs=pl.BlockSpec((count, 2 * (rows // count), half), lambda f: (0, 0, 0)),
-        scratch_shapes=[pltpu.VMEM((rows, features), jnp.float32)],
+        out_specs=pl.BlockSpec(out_shape, lambda f: (0, 0, 0)),
+        scratch_shapes=[
+            pltpu.VMEM((rows, features), jnp.bfloat16),
+            pltpu.VMEM((rows, features), jnp.bfloat16),
+            pltpu.VMEM((rows, features), jnp.float32),
+        ],
         compiler_params=pltpu.CompilerParams(vmem_limit_bytes=60 * 2**20),
-    )(x, g, gate, up, down)
+    )(arrived, gate, up, down)
 
 
 def normalize(residual, norm_gain):
@@ -237,12 +358,7 @@
         axis=0,
     )
     meta = jnp.pad(meta, ((0, 3), (0, 128 - token_count)))
-    tokens, metas, key_states = exchange(
-        "ctx",
-        0,
-        [jnp.concatenate([expert_input, out_grad], axis=0), meta, key_state],
-        ("gather", "gather", "gather"),
-    )
+    metas, key_states = exchange("ctx", 0, [meta, key_state], ("gather", "gather"))
 
     choice = metas[:, 0:2, :token_count].astype(jnp.int32)
     choice_by_token = jnp.transpose(choice, (0, 2, 1)).reshape(-1)
@@ -267,33 +383,28 @@
     row_scale = jnp.concatenate(
         [jnp.ones((exp_count, depth), jnp.float32), slot_weight.reshape(exp_count, depth)], axis=1
     )
-    outgoing = jnp.dot(
+    arrived = relay(
+        ("ctx", "exp"),
+        1,
+        "gather",
+        features // 4,
+        jnp.concatenate([expert_input, out_grad], axis=0),
         pick_both.astype(jnp.bfloat16),
-        tokens.reshape(2 * all_tokens, features),
-        preferred_element_type=jnp.float32,
-    )
-    outgoing = (outgoing * row_scale.reshape(-1, 1)).astype(jnp.bfloat16)
-    [arrived] = exchange(
-        "exp", 1, [outgoing.reshape(exp_count, 2 * depth, features)], ("swap",)
-    )
-    partials = expert_rows(
-        arrived[:, :depth].reshape(slots, features),
-        arrived[:, depth:].reshape(slots, features),
-        expert_gate,
-        expert_up,
-        expert_down,
-        exp_count,
-    )
-    [returned] = exchange("exp", 2, [partials], ("swap",))
+        row_scale.reshape(-1, 1),
+    )
+    partials = expert_rows(arrived, expert_gate, expert_up, expert_down)
 
     back = jnp.transpose(pick, (2, 3, 0, 1))[:, None, :, :, None, :]
     halves = jnp.eye(2, dtype=jnp.float32)[None, :, None, None, :, None]
     merge = (back * halves).reshape(2 * all_tokens, 2 * slots).astype(jnp.bfloat16)
-    sums = jnp.dot(
-        merge, returned.reshape(2 * slots, half), preferred_element_type=jnp.float32
-    ).astype(jnp.bfloat16)
-    [groups] = exchange(
-        "ctx", 3, [sums.reshape(ctx_count, 2 * token_count, half)], ("swap",)
+    groups = relay(
+        ("exp", "ctx"),
+        2,
+        "swap",
+        half // 3,
+        partials,
+        merge,
+        jnp.ones((2 * all_tokens, 1), jnp.float32),
     )
 
     def split(a):

time: 211 us -> 174 us (0.82)
  Pallas kernels: 172 us -> 148 us
  matrix products: 13 us -> 6.91 us
  other arithmetic: 12.9 us -> 8.38 us
    pallas_call x6 -> x3, Pallas kernels: 148 us -> 36.6 us  [exchange(): pl.pallas_call(functools.partial(exchange_kernel, axis, n, kinds), out_sh...]
    pallas_call x0 -> x2, Pallas kernels: none -> 87.5 us  [relay(): pl.pallas_call(functools.partial(relay_kernel, axes, counts, kind, width)...]
    dot_general x2 -> x0, matrix products: 6.13 us -> none  [the longest x1 3.14 us: body(): jnp.dot(pick_both.astype(jnp.bfloat16), tokens.reshape(2 * all_tokens, fe...]
    slice x1 -> x0, local copies, waits for them, and re-layouts: 4.36 us -> none  [body(): arrived[:, depth:].reshape(slots, features)]
where the time goes in v2:
time: 174 us; the launch traced here: 173 us
  Pallas kernels  148 us (85%)
  local copies, waits for them, and re-layouts  9.32 us (5%)
  other arithmetic  8.38 us (5%)
  matrix products  6.91 us (4%)
    pallas_call x2, Pallas kernels, relay(): pl.pallas_call(functools.partial(relay_kernel, axes, counts, kind, width)...  87.5 us
    pallas_call x3, Pallas kernels, exchange(): pl.pallas_call(functools.partial(exchange_kernel, axis, n, kinds), out_sh...  36.6 us
    pallas_call x1, Pallas kernels, expert_rows(): pl.pallas_call(expert_kernel, grid=(hidden // tile,), out_shape=jax.Shape...  23.7 us

profile of v2, /device:TPU:0, one launch (start us, length us, event | category | flops | bytes accessed | tf_op | source)
XLA Modules:
  0.0 173.4 jit_solution(5316050821169495292)
XLA Ops:
  0.6 0.8 select_reduce_fusion.1
  1.4 0.6 slice.39
  2.0 0.7 fusion.41
  2.7 1.8 %fusion.32.refs_1_ = f32[128,128]{1,0:T(8,128)} fusion(bf16[192,128]{1,0:T(8,128)(2,1)S(1)} %copy-done, bf16[192,128]{1,0:T(8,128)(2,1)} %param.14, f32[192]{0:T(256)S(1)} %get-tuple-element.21), kind=kOutput, calls=%fused_computation.66 | convolution fusion | flops 37797888 | bytes 164608 | tf_op jit(solution)/shard_map/dot_general | solution.py:271
  4.5 0.7 pad.16.clone
  5.2 0.7 convert_bitcast_fusion.1
  5.9 0.7 maximum_maximum_fusion
  6.6 0.6 pad.9.refs_0_
  7.2 11.1 %shard_map.148 = (f32[4,8,128]{2,1,0:T(8,128)}, f32[4,128,128]{2,1,0:T(8,128)}) custom-call(f32[8,128]{1,0:T(8,128)} %pad.9.refs_0_, f32[128,128]{1,0:T(8,128)} %fusion.32.refs_1_), custom_call_target="tpu_custom_call" | custom-call | tf_op jit(solution)/shard_map/pallas_call | solution.py:64
  18.3 0.8 slice_bitcast_fusion.4
  19.2 0.1 eq.52
  19.3 0.2 convert_reduce_fusion.2
  19.7 0.1 mul.229
  19.8 0.1 select_reduce_fusion
  20.1 0.2 reshape.139.scale
  20.3 0.1 reduce_sum.97
  20.5 0.7 multiply_add_fusion
  21.2 0.2 convert_reduce_fusion.1
  21.5 0.2 fusion.16
  21.6 0.5 copy.31
  22.2 0.4 reshape.138.mat
  22.5 0.1 fusion.20
  22.9 53.7 %shard_map.149.rows_ref = bf16[8,80,3072]{2,1,0:T(8,128)(2,1)S(1)} custom-call(bf16[48,3072]{1,0:T(8,128)(2,1)S(1)} %pad_maximum_fusion.1.src, bf16[640,192]{1,0:T(8,128)(2,1)S(1)} %reshape.138.mat, f32[640,1]{1,0:T(8,128)S(1)} %reshape.139.scale), custom_call_target="tpu_custom_call" | custom-call | tf_op jit(solution)/shard_map/pallas_call | solution.py:161
  76.6 1.9 %copy-done.1 = bf16[8,80,3072]{2,1,0:T(8,128)(2,1)} copy-done((bf16[8,80,3072]{2,1,0:T(8,128)(2,1)}, bf16[8,80,3072]{2,1,0:T(8,128)(2,1)S(1)}, u32[]{:S(2)}) %copy-start.1) | copy-done | bytes 3932184
  78.5 23.7 %shard_map.150.src = bf16[8,80,1536]{2,1,0:T(8,128)(2,1)} custom-call(bf16[8,80,3072]{2,1,0:T(8,128)(2,1)} %copy-done.1, bf16[1,3072,1152]{2,1,0:T(8,128)(2,1)} %gate_ref.1, bf16[1,3072,1152]{2,1,0:T(8,128)(2,1)} %up_ref.1, bf16[1,1152,3072]{2,1,0:T(8,128)(2,1)} %down_ref.1), custom_call_target="tpu_custom_call" | custom-call | tf_op jit(solution)/shard_map/pallas_call | solution.py:238
  102.2 0.2 copy.30
  102.5 0.6 multiply_convert_fusion
  103.0 0.8 convert_element_type.90.mat
  103.9 33.8 %shard_map.151 = bf16[4,48,1536]{2,1,0:T(8,128)(2,1)S(1)} custom-call(bf16[8,80,1536]{2,1,0:T(8,128)(2,1)S(1)} %copy-done.2, bf16[192,640]{1,0:T(8,128)(2,1)S(1)} %convert_element_type.90.mat, f32[192,1]{1,0:T(8,128)S(1)} %broadcast_in_dim.44.scale), custom_call_target="tpu_custom_call" | custom-call | tf_op jit(solution)/shard_map/pallas_call | solution.py:161
  137.9 0.2 multiply_reduce_fusion
  138.2 0.8 fusion.24.refs_0_
  139.0 15.6 %shard_map.152 = bf16[8,48,1536]{2,1,0:T(8,128)(2,1)} custom-call(bf16[48,1536]{1,0:T(8,128)(2,1)} %fusion.24.refs_0_), custom_call_target="tpu_custom_call" | custom-call | tf_op jit(solution)/shard_map/pallas_call | solution.py:64
  154.6 1.3 fusion.40
  156.0 0.3 fusion.18
  156.3 0.3 fusion.10
  156.6 0.1 copy-done.8
  156.7 1.0 convolution_multiply_fusion.5.refs_0_
  157.7 9.9 %shard_map.153 = f32[4,128,128]{2,1,0:T(8,128)} custom-call(f32[128,128]{1,0:T(8,128)} %convolution_multiply_fusion.5.refs_0_), custom_call_target="tpu_custom_call" | custom-call | tf_op jit(solution)/shard_map/pallas_call | solution.py:64
  167.7 0.8 slice_reduce_fusion
  168.5 0.2 select_reduce_fusion.2
  168.7 1.0 multiply_reduce_fusion.1
  169.8 0.4 fusion.9
  170.2 0.8 fusion.13
  171.0 0.2 fusion.2
  171.2 0.2 fusion.43
  171.4 0.9 fusion.12
  172.3 0.1 fusion.42
  172.5 0.8 fusion.11
  (44 shorter events, 1.1 us)
Async XLA Ops:
  0.6 2.1 %copy-start = (bf16[192,128]{1,0:T(8,128)(2,1)S(1)}, bf16[192,128]{1,0:T(8,128)(2,1)}, u32[]{:S(2)}) copy-start(bf16[192,128]{1,0:T(8,128)(2,1)} %param.15) | copy-start | bytes 147460
  21.4 1.1 copy-start.5
  21.4 1.3 copy-start.9
  21.5 1.4 copy-start.4
  76.6 1.9 %copy-start.1 = (bf16[8,80,3072]{2,1,0:T(8,128)(2,1)}, bf16[8,80,3072]{2,1,0:T(8,128)(2,1)S(1)}, u32[]{:S(2)}) copy-start(bf16[8,80,3072]{2,1,0:T(8,128)(2,1)S(1)} %shard_map.149.rows_ref) | copy-start | bytes 11796484
  102.2 1.7 copy-start.2
  139.0 16.9 %copy-start.3 = (bf16[128,3072]{1,0:T(8,128)(2,1)S(1)}, bf16[128,3072]{1,0:T(8,128)(2,1)}, u32[]{:S(2)}) copy-start(bf16[128,3072]{1,0:T(8,128)(2,1)} %param.22) | copy-start | bytes 2359300
  155.9 0.8 copy-start.8
  155.9 13.8 %copy-start.6 = (bf16[192,128]{1,0:T(8,128)(2,1)S(1)}, bf16[192,128]{1,0:T(8,128)(2,1)}, u32[]{:S(2)}) copy-start(bf16[192,128]{1,0:T(8,128)(2,1)} %param.14) | copy-start | bytes 147460
  156.6 15.8 %copy-start.7 = (f32[4,128,128]{2,1,0:T(8,128)S(1)}, f32[4,128,128]{2,1,0:T(8,128)}, u32[]{:S(2)}) copy-start(f32[4,128,128]{2,1,0:T(8,128)} %get-tuple-element.6) | copy-start | bytes 786436

commit v3 on v2

--- a/solution.py
+++ b/solution.py
@@ -358,7 +358,7 @@
         axis=0,
     )
     meta = jnp.pad(meta, ((0, 3), (0, 128 - token_count)))
-    metas, key_states = exchange("ctx", 0, [meta, key_state], ("gather", "gather"))
+    metas, key_states = exchange("ctx", 0, [meta, key_state.astype(jnp.bfloat16)], ("gather", "gather"))
 
     choice = metas[:, 0:2, :token_count].astype(jnp.int32)
     choice_by_token = jnp.transpose(choice, (0, 2, 1)).reshape(-1)
@@ -387,7 +387,7 @@
         ("ctx", "exp"),
         1,
         "gather",
-        features // 4,
+        features // 6,
         jnp.concatenate([expert_input, out_grad], axis=0),
         pick_both.astype(jnp.bfloat16),
         row_scale.reshape(-1, 1),
@@ -401,7 +401,7 @@
         ("exp", "ctx"),
         2,
         "swap",
-        half // 3,
+        half // 4,
         partials,
         merge,
         jnp.ones((2 * all_tokens, 1), jnp.float32),
@@ -431,7 +431,7 @@
         (((0,), (0,)), ((), ())),
         precision=lax.Precision.HIGHEST,
     )
-    [adjoints] = exchange("ctx", 5, [adjoint], ("gather",))
+    [adjoints] = exchange("ctx", 5, [adjoint.astype(jnp.bfloat16)], ("gather",))
 
     totals = metas[:, 4, 0]
     place = jnp.arange(ctx_count, dtype=jnp.int32)
@@ -441,8 +441,8 @@
     decay = jnp.exp(jnp.sum(jnp.where(between, totals[None, :], 0.0), axis=1))
     before = jnp.where(place < ctx_place, decay, 0.0)
     after = jnp.where(place > ctx_place, decay, 0.0)
-    state_in = jnp.sum(before[:, None, None] * key_states, axis=0)
-    adjoint_out = jnp.sum(after[:, None, None] * adjoints, axis=0)
+    state_in = jnp.sum(before[:, None, None] * key_states.astype(jnp.float32), axis=0)
+    adjoint_out = jnp.sum(after[:, None, None] * adjoints.astype(jnp.float32), axis=0)
     return block_grads(
         query_rows, key_rows, value_rows, attn_grad, levels, state_in, adjoint_out, score_scale
     )

time: 174 us -> 166 us (0.954)
  Pallas kernels: 148 us -> 139 us
    pallas_call x2, Pallas kernels: 87.5 us -> 83.3 us  [relay(): pl.pallas_call(functools.partial(relay_kernel, axes, counts, kind, width)...]
    pallas_call x3, Pallas kernels: 36.6 us -> 32.4 us  [exchange(): pl.pallas_call(functools.partial(exchange_kernel, axis, n, kinds), out_sh...]
where the time goes in v3:
time: 166 us; the launch traced here: 165 us
  Pallas kernels  139 us (84%)
  local copies, waits for them, and re-layouts  9.32 us (6%)
  other arithmetic  8.35 us (5%)
  matrix products  6.9 us (4%)
    pallas_call x2, Pallas kernels, relay(): pl.pallas_call(functools.partial(relay_kernel, axes, counts, kind, width)...  83.3 us
    pallas_call x3, Pallas kernels, exchange(): pl.pallas_call(functools.partial(exchange_kernel, axis, n, kinds), out_sh...  32.4 us
    pallas_call x1, Pallas kernels, expert_rows(): pl.pallas_call(expert_kernel, grid=(hidden // tile,), out_shape=jax.Shape...  23.7 us

profile of v3, /device:TPU:0, one launch (start us, length us, event | category | flops | bytes accessed | tf_op | source)
XLA Modules:
  0.0 165.0 jit_solution(5726687608994444569)
XLA Ops:
  0.6 0.8 select_reduce_fusion.1
  1.4 0.6 slice.39
  2.0 0.7 fusion.41
  2.7 1.8 %convolution_convert_fusion.refs_1_ = bf16[128,128]{1,0:T(8,128)(2,1)} fusion(bf16[192,128]{1,0:T(8,128)(2,1)S(1)} %copy-done, bf16[192,128]{1,0:T(8,128)(2,1)} %param.14, f32[192]{0:T(256)S(1)} %get-tuple-element.21), kind=kOutput, calls=%fused_computation.24 | convolution fusion | flops 37814272 | bytes 131840 | tf_op jit(solution)/shard_map/dot_general | solution.py:271
  4.5 0.7 pad.16.clone
  5.2 0.7 convert_bitcast_fusion.1
  5.9 0.7 maximum_maximum_fusion
  6.6 0.6 pad.9.refs_0_
  7.2 9.2 %shard_map.148 = (f32[4,8,128]{2,1,0:T(8,128)}, bf16[4,128,128]{2,1,0:T(8,128)(2,1)}) custom-call(f32[8,128]{1,0:T(8,128)} %pad.9.refs_0_, bf16[128,128]{1,0:T(8,128)(2,1)} %convolution_convert_fusion.refs_1_), custom_call_target="tpu_custom_call" | custom-call | tf_op jit(solution)/shard_map/pallas_call | solution.py:64
  16.5 0.8 slice_bitcast_fusion.4
  17.4 0.1 eq.52
  17.5 0.2 convert_reduce_fusion.2
  17.8 0.1 mul.229
  17.9 0.1 select_reduce_fusion
  18.2 0.2 reshape.139.scale
  18.4 0.1 reduce_sum.97
  18.6 0.7 multiply_add_fusion
  19.4 0.2 convert_reduce_fusion.1
  19.6 0.2 fusion.17
  19.8 0.5 copy.31
  20.3 0.4 reshape.138.mat
  20.7 0.1 fusion.21
  21.0 51.6 %shard_map.149.rows_ref = bf16[8,80,3072]{2,1,0:T(8,128)(2,1)S(1)} custom-call(bf16[48,3072]{1,0:T(8,128)(2,1)S(1)} %pad_maximum_fusion.1.src, bf16[640,192]{1,0:T(8,128)(2,1)S(1)} %reshape.138.mat, f32[640,1]{1,0:T(8,128)S(1)} %reshape.139.scale), custom_call_target="tpu_custom_call" | custom-call | tf_op jit(solution)/shard_map/pallas_call | solution.py:161
  72.7 1.9 %copy-done.1 = bf16[8,80,3072]{2,1,0:T(8,128)(2,1)} copy-done((bf16[8,80,3072]{2,1,0:T(8,128)(2,1)}, bf16[8,80,3072]{2,1,0:T(8,128)(2,1)S(1)}, u32[]{:S(2)}) %copy-start.1) | copy-done | bytes 3932184
  74.5 23.7 %shard_map.150.src = bf16[8,80,1536]{2,1,0:T(8,128)(2,1)} custom-call(bf16[8,80,3072]{2,1,0:T(8,128)(2,1)} %copy-done.1, bf16[1,3072,1152]{2,1,0:T(8,128)(2,1)} %gate_ref.1, bf16[1,3072,1152]{2,1,0:T(8,128)(2,1)} %up_ref.1, bf16[1,1152,3072]{2,1,0:T(8,128)(2,1)} %down_ref.1), custom_call_target="tpu_custom_call" | custom-call | tf_op jit(solution)/shard_map/pallas_call | solution.py:238
  98.2 0.2 copy.30
  98.5 0.6 multiply_convert_fusion
  99.1 0.8 convert_element_type.103.mat
  100.0 31.7 %shard_map.151 = bf16[4,48,1536]{2,1,0:T(8,128)(2,1)S(1)} custom-call(bf16[8,80,1536]{2,1,0:T(8,128)(2,1)S(1)} %copy-done.2, bf16[192,640]{1,0:T(8,128)(2,1)S(1)} %convert_element_type.103.mat, f32[192,1]{1,0:T(8,128)S(1)} %broadcast_in_dim.44.scale), custom_call_target="tpu_custom_call" | custom-call | tf_op jit(solution)/shard_map/pallas_call | solution.py:161
  131.8 0.2 multiply_reduce_fusion
  132.2 0.8 fusion.25.refs_0_
  133.0 16.6 %shard_map.152 = bf16[8,48,1536]{2,1,0:T(8,128)(2,1)} custom-call(bf16[48,1536]{1,0:T(8,128)(2,1)} %fusion.25.refs_0_), custom_call_target="tpu_custom_call" | custom-call | tf_op jit(solution)/shard_map/pallas_call | solution.py:64
  149.6 1.3 fusion.40
  150.9 0.3 fusion.19
  151.2 0.3 fusion.10
  151.6 0.1 copy-done.7
  151.7 1.0 fusion.14.refs_0_
  152.7 6.6 %shard_map.153 = bf16[4,128,128]{2,1,0:T(8,128)(2,1)} custom-call(bf16[128,128]{1,0:T(8,128)(2,1)} %fusion.14.refs_0_), custom_call_target="tpu_custom_call" | custom-call | tf_op jit(solution)/shard_map/pallas_call | solution.py:64
  159.3 0.8 slice_reduce_fusion
  160.1 0.2 select_reduce_fusion.2
  160.3 1.0 multiply_reduce_fusion.1
  161.3 0.4 fusion.9
  161.7 0.8 fusion.13
  162.6 0.2 fusion.2
  162.8 0.2 fusion.43
  163.0 0.9 fusion.12
  163.8 0.1 fusion.42
  164.1 0.8 fusion.11
  (44 shorter events, 1.1 us)
Async XLA Ops:
  0.6 2.1 %copy-start = (bf16[192,128]{1,0:T(8,128)(2,1)S(1)}, bf16[192,128]{1,0:T(8,128)(2,1)}, u32[]{:S(2)}) copy-start(bf16[192,128]{1,0:T(8,128)(2,1)} %param.15) | copy-start | bytes 147460
  19.5 1.1 copy-start.5
  19.6 1.3 copy-start.9
  19.6 1.4 copy-start.4
  72.7 1.9 %copy-start.1 = (bf16[8,80,3072]{2,1,0:T(8,128)(2,1)}, bf16[8,80,3072]{2,1,0:T(8,128)(2,1)S(1)}, u32[]{:S(2)}) copy-start(bf16[8,80,3072]{2,1,0:T(8,128)(2,1)S(1)} %shard_map.149.rows_ref) | copy-start | bytes 11796484
  98.2 1.7 %copy-start.2 = (bf16[8,80,1536]{2,1,0:T(8,128)(2,1)S(1)}, bf16[8,80,1536]{2,1,0:T(8,128)(2,1)}, u32[]{:S(2)}) copy-start(bf16[8,80,1536]{2,1,0:T(8,128)(2,1)} %shard_map.150.src) | copy-start | bytes 5898244
  133.0 17.9 %copy-start.3 = (bf16[128,3072]{1,0:T(8,128)(2,1)S(1)}, bf16[128,3072]{1,0:T(8,128)(2,1)}, u32[]{:S(2)}) copy-start(bf16[128,3072]{1,0:T(8,128)(2,1)} %param.22) | copy-start | bytes 2359300
  150.9 0.8 copy-start.7
  150.9 10.4 %copy-start.6 = (bf16[192,128]{1,0:T(8,128)(2,1)S(1)}, bf16[192,128]{1,0:T(8,128)(2,1)}, u32[]{:S(2)}) copy-start(bf16[192,128]{1,0:T(8,128)(2,1)} %param.14) | copy-start | bytes 147460
  151.2 12.8 %copy-start.8 = (bf16[4,128,128]{2,1,0:T(8,128)(2,1)S(1)}, bf16[4,128,128]{2,1,0:T(8,128)(2,1)}, u32[]{:S(2)}) copy-start(bf16[4,128,128]{2,1,0:T(8,128)(2,1)} %get-tuple-element.6) | copy-start | bytes 393220
